TPU v7x, 256 devices: a whole 4x4x8 slice. The times are simulated.
256 devices in a mesh: ctx: 64 (over x, z_lo, y), chan: 4 (over z_hi, core).
Axes of the slice: x: 4, y: 4, z: 8 (z_hi: 2, z_lo: 4; z = z_hi * 4 + z_lo), core: 2. Of those that a mesh axis runs over, the one named last changes fastest.
Arguments:
- token_ids: int32 [16384], P('ctx'), may hold values from 0 to 511
- domain_ids: int32 [16384], P('ctx'), may hold values from 0 to 7
- domain_counts: int32 [64, 8], P('ctx'), may hold values from 16 to 141, as said below
- embed_table: bfloat16 [512, 4096], P(None, 'chan'), may hold values from -6 to 6
- query_act: bfloat16 [4096, 16384], P('chan', 'ctx'), may hold values from -6 to 6
- key_act: bfloat16 [4096, 16384], P('chan', 'ctx'), may hold values from -6 to 6
- conv_saved: bfloat16 [4096, 16384], P('chan', 'ctx'), may hold values from -6 to 6
- loss_seed: bfloat16 [4096, 16384], P('chan', 'ctx'), may hold values from -6 to 6
- filters: float32 [4096, 16384], P('chan', 'ctx')
- skip_gain: float32 [4096], P('chan'), may hold values from 0.5 to 1.5
Outputs:
- grad_query: float32 [4096, 16384], P('chan', 'ctx')
- grad_key: float32 [4096, 16384], P('chan', 'ctx')
- grad_value: float32 [4096, 16384], P('chan', 'ctx')
- grad_filter: float32 [4096, 16384], P('chan', 'ctx')
Inputs may be any that keep to these rules, and one draw needn't show every extreme that they name: `domain_counts`: each entry is a positive token count.
All inputs are finite; a program needn't handle non-finite values.
Results may differ from a plain program's by a relative error of at most 0.0028.
Values sent between devices are 32-bit elements; how exact they have to be, the bound alone decides.
A program may use at most 128 MiB of HBM per device.

v0:
```python
from functools import partial
import math

import jax
import jax.numpy as jnp
from jax import lax
from jax.sharding import PartitionSpec as P

count_unit = 64.0


def angles(number, period):
    turned = (number % period).astype(jnp.float32) * (2.0 * math.pi / period)
    return (jnp.cos(turned), jnp.sin(turned))


def rotate(form, real, imag, cosine, sine, sign):
    product = partial(jnp.einsum, form, precision=lax.Precision.HIGHEST)
    if imag is None:
        return (product(real, cosine), sign * product(real, sine))
    return (
        product(real, cosine) - sign * product(imag, sine),
        product(imag, cosine) + sign * product(real, sine),
    )


def ch_forward(signal):
    parts = lax.axis_size("ctx")
    count, chans, width = signal.shape
    span = 2 * parts
    whole = lax.all_to_all(
        signal.reshape(count, chans, 1, width), "ctx", split_axis=1, concat_axis=2, tiled=True
    )
    cosine, sine = angles(jnp.arange(parts)[:, None] * jnp.arange(span)[None, :], span)
    real, imag = rotate("mcjr,jk->mckr", whole, None, cosine, sine, -1.0)
    steps = jnp.arange(width)
    cosine, sine = angles(jnp.arange(span)[:, None] * steps[None, :], width * span)
    real, imag = (real * cosine + imag * sine, imag * cosine - real * sine)
    cosine, sine = angles(steps[:, None] * steps[None, :], width)
    return rotate("mckr,ra->mcka", real, imag, cosine, sine, -1.0)


def ch_inverse(real, imag, packed):
    parts = lax.axis_size("ctx")
    width = real.shape[3]
    span = 2 * parts
    steps = jnp.arange(width)
    cosine, sine = angles(steps[:, None] * steps[None, :], width)
    real, imag = rotate("mcka,ar->mckr", real, imag, cosine, sine, 1.0)
    cosine, sine = angles(jnp.arange(span)[:, None] * steps[None, :], width * span)
    real, imag = (real * cosine - imag * sine, imag * cosine + real * sine)
    cosine, sine = angles(jnp.arange(span)[:, None] * jnp.arange(parts)[None, :], span)
    product = partial(jnp.einsum, "mckr,kb->mcbr", precision=lax.Precision.HIGHEST)
    result = product(real, cosine) - product(imag, sine)
    result = result * (1.0 / (width * span))
    returned = lax.all_to_all(result, "ctx", split_axis=2, concat_axis=1, tiled=True)
    return returned[:, :, 0, :]


def on_device(
    token_ids,
    domain_ids,
    domain_counts,
    embed_table,
    query_act,
    key_act,
    conv_saved,
    loss_seed,
    filters,
    skip_gain,
):
    parts = lax.axis_size("ctx")
    width = query_act.shape[1]
    vocab_rows = embed_table.shape[0]
    domains = domain_counts.shape[1]
    onehot = (lax.broadcasted_iota(jnp.int32, (vocab_rows, width), 0) == token_ids[None, :]).astype(
        jnp.bfloat16
    )
    values = lax.dot_general(
        embed_table, onehot, (((0,), (0,)), ((), ())), preferred_element_type=jnp.float32
    )
    keyed = key_act.astype(jnp.float32)
    mixed = keyed * values
    totals = lax.psum(domain_counts.astype(jnp.float32), "ctx")
    picked = (lax.broadcasted_iota(jnp.int32, (domains, width), 0) == domain_ids[None, :]).astype(
        jnp.float32
    )
    weight = jnp.sum(picked * (count_unit * parts / totals[0])[:, None], axis=0)
    rounded = (loss_seed.astype(jnp.float32) * weight[None, :]).astype(jnp.bfloat16)
    upstream = lax.optimization_barrier(rounded).astype(jnp.float32)
    grad_query = upstream * conv_saved.astype(jnp.float32)
    dconv = upstream * query_act.astype(jnp.float32)
    forward, inverse = (ch_forward, ch_inverse)
    both_real, both_imag = forward(jnp.stack([mixed, filters]))
    seed_real, seed_imag = forward(dconv[None])
    zr, zi, hr, hi = (both_real[0], both_imag[0], both_real[1], both_imag[1])
    sr, si = (seed_real[0], seed_imag[0])
    back_r = hr * sr + hi * si
    back_i = hr * si - hi * sr
    filt_r = zr * sr + zi * si
    filt_i = zr * si - zi * sr
    outcome = inverse(jnp.stack([back_r, filt_r]), jnp.stack([back_i, filt_i]), False)
    back = outcome[0] + skip_gain[:, None] * dconv
    grad_filter = outcome[1] * (width * parts) ** (-0.5)
    return (grad_query, back * values, back * keyed, grad_filter)


def solution(mesh):
    in_specs = (
        P("ctx"),
        P("ctx"),
        P("ctx", None),
        P(None, "chan"),
        P("chan", "ctx"),
        P("chan", "ctx"),
        P("chan", "ctx"),
        P("chan", "ctx"),
        P("chan", "ctx"),
        P("chan"),
    )
    out_specs = (P("chan", "ctx"), P("chan", "ctx"), P("chan", "ctx"), P("chan", "ctx"))
    return jax.shard_map(
        on_device, mesh=mesh, in_specs=in_specs, out_specs=out_specs, check_vma=False
    )
```

profile of v0, /device:TPU:192, one launch (start us, length us, event | category | flops | bytes accessed | tf_op | source)
XLA Modules:
  0.0 380.0 jit_solution(17053955357574867612)
XLA Ops:
  2.7 165.7 %psum.7 = f32[1,8]{1,0:T(1,128)S(1)} all-reduce(f32[1,8]{1,0:T(1,128)S(1)} %convert_element_type.97), channel_id=1, replica_groups=mesh['ctx'=64,'chan'=4] {'ctx'}, use_global_device_ids=true, to_apply=%region_0.0 | all-reduce | flops 8 | bytes 64 | tf_op jit(solution)/shard_map/psum | solution.py:84
  169.7 1.9 copy.64
  171.6 28.8 %all-to-all-start.1 = ((f32[1,1024,1,256]{3,2,0,1:T(1,128)}), f32[1,1024,1,256]{3,2,0,1:T(1,128)}, u32[]{:S(2)}, u32[]{:S(2)}) async-start(f32[1,1024,1,256]{3,2,0,1:T(1,128)} %copy.64), calls=%async_computation.1 | async-start | bytes 2097152 | tf_op jit(solution)/shard_map/all_to_all | solution.py:31
  204.5 2.3 copy.60
  206.8 23.2 %all-to-all-done.1 = f32[1,1024,1,256]{3,2,0,1:T(1,128)} async-done(((f32[1,1024,1,256]{3,2,0,1:T(1,128)}), f32[1,1024,1,256]{3,2,0,1:T(1,128)}, u32[]{:S(2)}, u32[]{:S(2)}) %all-to-all-start.1) | async-done | bytes 1048608 | tf_op jit(solution)/shard_map/all_to_all | solution.py:31
  230.0 9.6 %all-to-all-start = ((f32[2,1024,1,256]{3,0,2,1:T(2,128)}), f32[2,1024,1,256]{3,0,2,1:T(2,128)}, u32[]{:S(2)}, u32[]{:S(2)}) async-start(f32[2,1024,1,256]{3,0,2,1:T(2,128)} %copy.60), calls=%async_computation | async-start | bytes 4194304 | tf_op jit(solution)/shard_map/all_to_all | solution.py:31
  242.5 2.4 fusion.57
  244.9 2.4 fusion.59
  247.4 3.0 fusion.32
  250.4 4.5 %fusion.30 = f32[16,128,256]{2,1,0:T(8,128)} fusion(f32[128,16,256]{2,0,1:T(8,128)S(1)} %fusion.57, f32[128,16,256]{2,0,1:T(8,128)S(1)} %fusion.59, f32[128,256]{1,0:T(8,128)S(1)} %get-tuple-element.29, f32[128,256]{1,0:T(8,128)S(1)} %get-tuple-element.30), kind=kOutput, calls=%fused_computation.37 | convolution fusion | flops 1613103104 | bytes 6553600 | tf_op jit(solution)/shard_map/mckr,ra->mcka/dot_general | solution.py:23
  254.9 4.3 %multiply_subtract_fusion.2 = f32[16,128,256]{2,1,0:T(8,128)} fusion(f32[16,128,256]{2,1,0:T(8,128)S(1)} %fusion.32, f32[128,16,256]{2,0,1:T(8,128)S(1)} %fusion.57, f32[128,16,256]{2,0,1:T(8,128)S(1)} %fusion.59, f32[128,256]{1,0:T(8,128)S(1)} %fusion.108, f32[128,256]{1,0:T(8,128)S(1)} %broadcast_multiply_fusion), kind=kOutput, calls=%fused_computation.66 | convolution fusion | flops 1614151680 | bytes 8650752 | tf_op jit(solution)/shard_map/mckr,ra->mcka/dot_general | solution.py:22
  259.2 7.7 %all-to-all-done = f32[2,1024,1,256]{3,0,2,1:T(2,128)} async-done(((f32[2,1024,1,256]{3,0,2,1:T(2,128)}), f32[2,1024,1,256]{3,0,2,1:T(2,128)}, u32[]{:S(2)}, u32[]{:S(2)}) %all-to-all-start) | async-done | bytes 2097184 | tf_op jit(solution)/shard_map/all_to_all | solution.py:31
  266.9 6.3 %fusion.40 = f32[128,2,16,256]{3,0,2,1:T(8,128)S(1)} fusion(f32[2,64,16,1,256]{4,0,2,1,3:T(2,128)} %bitcast.9), kind=kOutput, calls=%fused_computation.55 | convolution fusion | flops 805421056 | bytes 6291456 | tf_op jit(solution)/shard_map/mcjr,jk->mckr/dot_general | solution.py:20
  273.2 6.6 %fusion.42 = f32[128,2,16,256]{3,0,2,1:T(8,128)S(1)} fusion(f32[2,64,16,1,256]{4,0,2,1,3:T(2,128)} %bitcast.9), kind=kOutput, calls=%fused_computation.57 | convolution fusion | flops 805421056 | bytes 6291456 | tf_op jit(solution)/shard_map/mcjr,jk->mckr/dot_general | solution.py:20
  279.8 4.8 %fusion.2 = f32[2,16,128,256]{3,2,1,0:T(8,128)S(1)} fusion(f32[128,2,16,256]{3,0,2,1:T(8,128)S(1)} %fusion.42, f32[128,2,16,256]{3,0,2,1:T(8,128)S(1)} %fusion.40, f32[128,256]{1,0:T(8,128)S(1)} %fusion.108, f32[128,256]{1,0:T(8,128)S(1)} %copy-done.7), kind=kOutput, calls=%fused_computation.4 | convolution fusion | flops 3225288704 | bytes 12845056 | tf_op jit(solution)/shard_map/mckr,ra->mcka/dot_general | solution.py:22
  284.7 4.9 %fusion = f32[2,16,128,256]{3,2,1,0:T(8,128)S(1)} fusion(f32[128,2,16,256]{3,0,2,1:T(8,128)S(1)} %fusion.42, f32[128,2,16,256]{3,0,2,1:T(8,128)S(1)} %fusion.40, f32[128,256]{1,0:T(8,128)S(1)} %fusion.108, f32[128,256]{1,0:T(8,128)S(1)} %copy-done.7), kind=kOutput, calls=%fused_computation.2 | convolution fusion | flops 3225288704 | bytes 12845056 | tf_op jit(solution)/shard_map/mckr,ra->mcka/dot_general | solution.py:23
  289.6 5.4 %multiply_subtract_fusion = f32[2,16,128,256]{3,2,1,0:T(8,128)S(1)} fusion(f32[2,16,128,256]{3,2,1,0:T(8,128)S(1)} %fusion.2, f32[128,2,16,256]{3,0,2,1:T(8,128)S(1)} %fusion.40, f32[128,2,16,256]{3,0,2,1:T(8,128)S(1)} %fusion.42, f32[128,256]{1,0:T(8,128)S(1)} %get-tuple-element.29, f32[128,256]{1,0:T(8,128)S(1)} %get-tuple-element.30), kind=kOutput, calls=%fused_computation.19 | convolution fusion | flops 3227385856 | bytes 17039360 | tf_op jit(solution)/shard_map/mckr,ra->mcka/dot_general | solution.py:22
  295.0 4.9 %multiply_add_fusion = f32[2,16,128,256]{3,2,1,0:T(8,128)S(1)} fusion(f32[2,16,128,256]{3,2,1,0:T(8,128)S(1)} %fusion, f32[128,2,16,256]{3,0,2,1:T(8,128)S(1)} %fusion.40, f32[128,2,16,256]{3,0,2,1:T(8,128)S(1)} %fusion.42, f32[128,256]{1,0:T(8,128)S(1)} %get-tuple-element.29, f32[128,256]{1,0:T(8,128)S(1)} %get-tuple-element.30), kind=kOutput, calls=%fused_computation.18 | convolution fusion | flops 3227385856 | bytes 17039360 | tf_op jit(solution)/shard_map/mckr,ra->mcka/dot_general | solution.py:23
  300.0 4.1 %fusion.26 = (f32[1,16,128,256]{3,2,1,0:T(8,128)S(1)}, f32[1,16,128,256]{3,2,1,0:T(8,128)S(1)}, f32[1,16,128,256]{3,2,1,0:T(8,128)S(1)}, f32[1,16,128,256]{3,2,1,0:T(8,128)S(1)}) fusion(f32[16,128,256]{2,1,0:T(8,128)S(1)} %copy-done.5, f32[2,16,128,256]{3,2,1,0:T(8,128)S(1)} %multiply_add_fusion, f32[2,16,128,256]{3,2,1,0:T(8,128)S(1)} %multiply_subtract_fusion, ...), kind=kOutput, calls=%fused_computation.33 | convolution fusion | flops 1620443136 | bytes 25427968 | tf_op jit(solution)/shard_map/mckr,ra->mcka/dot_general | solution.py:23
  304.1 4.6 %fusion.16 = f32[2,16,128,256]{3,2,1,0:T(8,128)S(1)} fusion(f32[1,16,128,256]{3,2,1,0:T(8,128)S(1)} %get-tuple-element.23, f32[1,16,128,256]{3,2,1,0:T(8,128)S(1)} %get-tuple-element.22), kind=kOutput, calls=%fused_computation.22 | convolution fusion | flops 3223191552 | bytes 8388608 | tf_op jit(solution)/shard_map/mcka,ar->mckr/dot_general | solution.py:23
  308.7 4.4 %fusion.17 = f32[2,16,128,256]{3,2,1,0:T(8,128)S(1)} fusion(f32[1,16,128,256]{3,2,1,0:T(8,128)S(1)} %get-tuple-element.23, f32[1,16,128,256]{3,2,1,0:T(8,128)S(1)} %get-tuple-element.22), kind=kOutput, calls=%fused_computation.23 | convolution fusion | flops 3223191552 | bytes 8388608 | tf_op jit(solution)/shard_map/mcka,ar->mckr/dot_general | solution.py:22
  313.1 4.7 %fusion.21 = f32[2,16,128,256]{3,2,1,0:T(8,128)S(1)} fusion(f32[2,16,128,256]{3,2,1,0:T(8,128)S(1)} %fusion.16, f32[1,16,128,256]{3,2,1,0:T(8,128)S(1)} %get-tuple-element.21, f32[1,16,128,256]{3,2,1,0:T(8,128)S(1)} %get-tuple-element.20), kind=kOutput, calls=%fused_computation.27 | convolution fusion | flops 3224240128 | bytes 12582912 | tf_op jit(solution)/shard_map/mcka,ar->mckr/dot_general | solution.py:23
  317.8 4.4 %fusion.20 = f32[2,16,128,256]{3,2,1,0:T(8,128)S(1)} fusion(f32[2,16,128,256]{3,2,1,0:T(8,128)S(1)} %fusion.17, f32[1,16,128,256]{3,2,1,0:T(8,128)S(1)} %get-tuple-element.21, f32[1,16,128,256]{3,2,1,0:T(8,128)S(1)} %get-tuple-element.20), kind=kOutput, calls=%fused_computation.26 | convolution fusion | flops 3224240128 | bytes 12582912 | tf_op jit(solution)/shard_map/mcka,ar->mckr/dot_general | solution.py:22
  322.2 2.9 fusion.8
  325.1 3.1 multiply_bitcast_fusion
  328.2 2.8 copy.66
  331.0 8.0 %all-to-all-start.2 = ((f32[2,16,64,256]{3,1,0,2:T(8,128)}), f32[2,16,64,256]{3,1,0,2:T(8,128)S(1)}, u32[]{:S(2)}, u32[]{:S(2)}) async-start(f32[2,16,64,256]{3,1,0,2:T(8,128)} %copy.66), calls=%async_computation.2 | async-start | bytes 4194304 | tf_op jit(solution)/shard_map/all_to_all | solution.py:56
  339.0 2.1 copy.57
  341.0 25.7 %all-to-all-done.2 = f32[2,16,64,256]{3,1,0,2:T(8,128)S(1)} async-done(((f32[2,16,64,256]{3,1,0,2:T(8,128)}), f32[2,16,64,256]{3,1,0,2:T(8,128)S(1)}, u32[]{:S(2)}, u32[]{:S(2)}) %all-to-all-start.2) | async-done | bytes 2097184 | tf_op jit(solution)/shard_map/all_to_all | solution.py:56
  368.5 2.7 copy.68
  371.2 3.3 convert_multiply_fusion
  374.5 2.7 copy.69
  (64 shorter events, 14.5 us)
Async XLA Ops:
  0.6 202.4 %copy-start = (bf16[512,1024]{1,0:T(8,128)(2,1)S(1)}, bf16[512,1024]{1,0:T(8,128)(2,1)}, u32[]{:S(2)}) copy-start(bf16[512,1024]{1,0:T(8,128)(2,1)} %param.13) | copy-start | bytes 3145732
  0.6 168.7 %copy-start.19 = (bf16[1024,256]{1,0:T(8,128)(2,1)S(1)}, bf16[1024,256]{1,0:T(8,128)(2,1)}, u32[]{:S(2)}) copy-start(bf16[1024,256]{1,0:T(8,128)(2,1)} %param.14) | copy-start | bytes 1572868
  169.3 2.3 copy-start.10
  169.6 2.1 copy-start.12
  171.6 30.1 %copy-start.18 = (f32[1024,256]{1,0:T(8,128)S(1)}, f32[1024,256]{1,0:T(8,128)}, u32[]{:S(2)}) copy-start(f32[1024,256]{1,0:T(8,128)} %param.18) | copy-start | bytes 3145732
  171.6 31.4 %copy-start.21 = (s32[256]{0:T(256)S(1)}, s32[256]{0:T(256)}, u32[]{:S(2)}) copy-start(s32[256]{0:T(256)} %param.10) | copy-start | bytes 3076
  171.6 58.4 %all-to-all-start.1 = ((f32[1,1024,1,256]{3,2,0,1:T(1,128)}), f32[1,1024,1,256]{3,2,0,1:T(1,128)}, u32[]{:S(2)}, u32[]{:S(2)}) async-start(f32[1,1024,1,256]{3,2,0,1:T(1,128)} %copy.64), calls=%async_computation.1 | async-start | bytes 2097152 | tf_op jit(solution)/shard_map/all_to_all | solution.py:31
  201.7 1.8 copy-start.8
  203.0 1.2 copy-start.16
  230.0 36.8 %all-to-all-start = ((f32[2,1024,1,256]{3,0,2,1:T(2,128)}), f32[2,1024,1,256]{3,0,2,1:T(2,128)}, u32[]{:S(2)}, u32[]{:S(2)}) async-start(f32[2,1024,1,256]{3,0,2,1:T(2,128)} %copy.60), calls=%async_computation | async-start | bytes 4194304 | tf_op jit(solution)/shard_map/all_to_all | solution.py:31
  240.7 14.2 %copy-start.6 = (f32[128,256]{1,0:T(8,128)}, f32[128,256]{1,0:T(8,128)S(1)}, u32[]{:S(2)}) copy-start(f32[128,256]{1,0:T(8,128)S(1)} %broadcast_multiply_fusion) | copy-start | bytes 393220
  247.4 7.5 %copy-start.2 = (f32[128,16,256]{2,0,1:T(8,128)}, f32[128,16,256]{2,0,1:T(8,128)S(1)}, u32[]{:S(2)}) copy-start(f32[128,16,256]{2,0,1:T(8,128)S(1)} %fusion.59) | copy-start | bytes 6291460
  273.2 6.6 %copy-start.7 = (f32[128,256]{1,0:T(8,128)S(1)}, f32[128,256]{1,0:T(8,128)}, u32[]{:S(2)}) copy-start(f32[128,256]{1,0:T(8,128)} %copy-done.6) | copy-start | bytes 393220
  295.0 4.9 %copy-start.3 = (f32[128,16,256]{2,0,1:T(8,128)S(1)}, f32[128,16,256]{2,0,1:T(8,128)}, u32[]{:S(2)}) copy-start(f32[128,16,256]{2,0,1:T(8,128)} %copy-done.2) | copy-start | bytes 6291460
  295.0 4.9 %copy-start.4 = (f32[16,128,256]{2,1,0:T(8,128)S(1)}, f32[16,128,256]{2,1,0:T(8,128)}, u32[]{:S(2)}) copy-start(f32[16,128,256]{2,1,0:T(8,128)} %fusion.30) | copy-start | bytes 6291460
  295.0 4.9 %copy-start.5 = (f32[16,128,256]{2,1,0:T(8,128)S(1)}, f32[16,128,256]{2,1,0:T(8,128)}, u32[]{:S(2)}) copy-start(f32[16,128,256]{2,1,0:T(8,128)} %multiply_subtract_fusion.2) | copy-start | bytes 6291460
  331.0 35.7 %all-to-all-start.2 = ((f32[2,16,64,256]{3,1,0,2:T(8,128)}), f32[2,16,64,256]{3,1,0,2:T(8,128)S(1)}, u32[]{:S(2)}, u32[]{:S(2)}) async-start(f32[2,16,64,256]{3,1,0,2:T(8,128)} %copy.66), calls=%async_computation.2 | async-start | bytes 4194304 | tf_op jit(solution)/shard_map/all_to_all | solution.py:56
  366.9 4.2 %copy-start.20 = (f32[1024]{0:T(1024)S(1)}, f32[1024]{0:T(1024)}, u32[]{:S(2)}) copy-start(f32[1024]{0:T(1024)} %param.19) | copy-start | bytes 12292
  368.5 2.7 copy-start.9
  368.5 2.7 copy-start.11
  368.5 2.7 copy-start.13
  368.5 2.7 copy-start.17
  374.4 2.7 copy-start.15
  374.4 4.0 %copy-start.14 = (f32[1024,256]{0,1:T(8,128)S(1)}, f32[1024,256]{0,1:T(8,128)}, u32[]{:S(2)}) copy-start(f32[1024,256]{0,1:T(8,128)} %get-tuple-element.24) | copy-start | bytes 3145732
  377.1 2.6 copy-start.1
where the time goes:
time: 388 us; the launch traced here: 380 us
  blocking collectives  166 us (43%)
  matrix products  78.3 us (20%)
  waiting for transfers between devices  56.5 us (15%)
  starting transfers between devices  46.4 us (12%)
  local copies, waits for them, and re-layouts  23.2 us (6%)
  other arithmetic  8.57 us (2%)
    psum x1, blocking collectives, on_device(): totals = lax.psum(domain_counts.astype(jnp.float32), 'ctx')  166 us
    all_to_all x2, starting transfers between devices, ch_forward(): lax.all_to_all(signal.reshape(count, chans, 1, width), 'ctx', split_axis=...  38.4 us
    all_to_all x2, waiting for transfers between devices, ch_forward(): lax.all_to_all(signal.reshape(count, chans, 1, width), 'ctx', split_axis=...  30.9 us
    all_to_all x1, waiting for transfers between devices, ch_inverse(): lax.all_to_all(result, 'ctx', split_axis=2, concat_axis=1, tiled=True)  25.7 us
    dot_general x4, matrix products, rotate(): return (product(real, cosine), sign * product(real, sine))  17.8 us
    dot_general x3, matrix products, rotate(): product(real, sine)  14.1 us
    dot_general x3, matrix products, rotate(): product(imag, sine)  13.6 us
    dot_general x3, matrix products, rotate(): product(imag, cosine) + sign * product(real, sine)  13.6 us
  transfers between devices with their start and end apart: 3, of which 3 were waited for; matrix products, arithmetic and copies ran while one was open for 7% of the time, Pallas kernels for 0%

commit v1 on v0

v1 whole, which is shorter than its diff:
```python
import functools

import jax
import jax.numpy as jnp
import ml_dtypes
import numpy as np
from jax import lax
from jax.experimental import pallas as pl
from jax.experimental.pallas import tpu as pltpu
from jax.sharding import PartitionSpec as P

MESH = pl.DeviceIdType.MESH
F32, BF16 = jnp.float32, jnp.bfloat16
count_unit = 64.0
LANES = 128
GROUP = 8
CHUNKS = 2


def split_host(x):
    high = x.astype(np.float32).astype(ml_dtypes.bfloat16)
    low = (x - high.astype(np.float64)).astype(np.float32).astype(ml_dtypes.bfloat16)
    return high, low


def constants(parts, width):
    total = parts * width
    j, r = np.arange(parts), np.arange(width)
    theta = 2.0 * np.pi * np.outer(j + 0.25, j) / parts
    first = np.concatenate([np.cos(theta), -np.sin(theta)], 0)
    phase = 2.0 * np.pi * np.outer(j + 0.25, r) / total
    turn = np.stack([np.cos(phase), np.sin(phase)]).astype(np.float32)
    omega = 2.0 * np.pi * (np.outer(r, r) % width) / width
    cosine, sine = np.cos(omega), np.sin(omega)
    inner = np.block([[cosine, -sine], [sine, cosine]])
    last = np.concatenate([np.cos(theta).T, np.sin(theta).T], 1) / total
    fh, fl = split_host(first)
    lh, ll = split_host(last)
    first_cat = np.concatenate([fh, fh, fl], 1)
    last_cat = np.concatenate([lh, lh, ll], 1)
    return first_cat, np.stack(split_host(inner)), last_cat, turn


def split(x):
    high = x.astype(BF16)
    return high, (x - high.astype(F32)).astype(BF16)


def dot(a, b):
    return jnp.dot(a, b, preferred_element_type=F32)


def turned(a, b, cosine, sine):
    return a * cosine + b * sine, b * cosine - a * sine


def kernel(
    parts, width,
    counts, tokens, domains, skip, first, last, turn,
    embed, query, key, loss, filters, inner,
    out, values_out, weight_out,
    cnt_src, cnt_all, embed_v, query_v, key_v, loss_v, inner_v, values_v,
    md, rf, rfh, rmd, res,
    load_sem, keep_sem, send_sem, recv_sem,
):
    me = lax.axis_index("ctx")
    chan = lax.axis_index("chan")
    rows = CHUNKS * GROUP
    halves = width // LANES
    tall = rows * halves
    barrier = pltpu.get_barrier_semaphore()

    def greet(k, carry):
        peer = lax.rem(me + k, parts)
        pl.semaphore_signal(barrier, inc=1, device_id=(peer, chan), device_id_type=MESH)
        return carry

    lax.fori_loop(1, parts, greet, 0)

    loads = [
        pltpu.make_async_copy(source, target, load_sem.at[i])
        for i, (source, target) in enumerate(
            [(embed, embed_v), (key, key_v), (query, query_v), (loss, loss_v), (inner, inner_v)]
        )
    ]
    for load in loads:
        load.start()
    cnt_src[...] = jnp.zeros_like(cnt_src)
    cnt_src[0:1, 0 : counts.shape[1]] = counts[...].astype(F32)

    def rows_of(ref, index):
        size = ref.shape[0] // parts
        return ref.at[pl.ds(pl.multiple_of(index * size, size), size)]

    def send(source, target, slot):
        own = pltpu.make_async_copy(rows_of(source, me), rows_of(target, me), recv_sem.at[slot])
        own.start()

        def go(k, carry):
            peer = lax.rem(me + k, parts)
            pltpu.make_async_remote_copy(
                src_ref=rows_of(source, peer),
                dst_ref=rows_of(target, me),
                send_sem=send_sem.at[slot],
                recv_sem=recv_sem.at[slot],
                device_id=(peer, chan),
                device_id_type=MESH,
            ).start()
            return carry

        lax.fori_loop(1, parts, go, 0)

    def arrived(target, slot):
        pltpu.make_async_copy(target, target, recv_sem.at[slot]).wait()

    def sent(target, slot):
        done = target.at[pl.ds(0, target.shape[0] // parts * (parts - 1))]
        pltpu.make_async_copy(done, done, send_sem.at[slot]).wait()

    pl.semaphore_wait(barrier, parts - 1)

    own = pltpu.make_async_copy(cnt_src, cnt_all.at[me], recv_sem.at[0])
    own.start()

    def tell(k, carry):
        peer = lax.rem(me + k, parts)
        pltpu.make_async_remote_copy(
            src_ref=cnt_src,
            dst_ref=cnt_all.at[me],
            send_sem=send_sem.at[0],
            recv_sem=recv_sem.at[0],
            device_id=(peer, chan),
            device_id_type=MESH,
        ).start()
        return carry

    lax.fori_loop(1, parts, tell, 0)
    send(filters, rf, 1)

    loads[0].wait()
    vocab = embed_v.shape[0]
    onehot = (
        lax.broadcasted_iota(jnp.int32, (vocab, width), 0) == tokens[...]
    ).astype(F32).astype(BF16)
    piece = 128

    def look_up(b, carry):
        at = pl.multiple_of(b * piece, piece)
        values_v[pl.ds(at, piece), :] = lax.dot_general(
            embed_v[:, pl.ds(at, piece)], onehot, (((0,), (0,)), ((), ())),
            preferred_element_type=F32,
        )
        return carry

    lax.fori_loop(0, values_v.shape[0] // piece, look_up, 0)
    keep = pltpu.make_async_copy(values_v, values_out, keep_sem)
    keep.start()
    for load in loads[1:4]:
        load.wait()
    arrived(cnt_all, 0)
    totals = jnp.sum(cnt_all[...], axis=0)[0:1, :]
    shares = (count_unit * parts) / totals
    weight = jnp.zeros((1, width), F32)
    for d in range(counts.shape[1]):
        weight = jnp.where(domains[...] == d, shares[0:1, d : d + 1], weight)
    weight_out[...] = weight

    def products(b, carry):
        at = pl.multiple_of(b * piece, piece)
        block = pl.ds(at, piece)
        mixed = key_v[block, :].astype(F32) * values_v[block, :]
        upstream = (loss_v[block, :].astype(F32) * weight).astype(BF16).astype(F32)
        dconv = upstream * query_v[block, :].astype(F32)
        for q in range(piece // rows):
            for chunk in range(CHUNKS):
                part = slice(q * rows + chunk * GROUP, q * rows + (chunk + 1) * GROUP)
                for h in range(halves):
                    start = pl.multiple_of((at + q * rows) * halves + h * GROUP, GROUP)
                    lanes = slice(h * LANES, (h + 1) * LANES)
                    md[chunk, pl.ds(start, GROUP), :] = mixed[part, lanes]
                    start = start + halves * GROUP
                    md[chunk, pl.ds(start, GROUP), :] = dconv[part, lanes]
        return carry

    lax.fori_loop(0, values_v.shape[0] // piece, products, 0)
    for chunk in range(CHUNKS):
        send(md.at[chunk], rmd.at[chunk], 2 + chunk)

    loads[4].wait()
    arrived(rf, 1)

    def halve(b, carry):
        at = pl.multiple_of(b * piece, piece)
        block = rf[pl.ds(at, piece), :]
        for q in range(piece // GROUP):
            for h in range(halves):
                start = pl.multiple_of((at + q * GROUP) * halves + h * GROUP, GROUP)
                rfh[pl.ds(start, GROUP), :] = block[
                    q * GROUP : (q + 1) * GROUP, h * LANES : (h + 1) * LANES
                ]
        return carry

    lax.fori_loop(0, rf.shape[0] // piece, halve, 0)

    def column(ref, start):
        return jnp.concatenate(
            [ref[pl.ds(start + h * GROUP, parts, stride=tall), :] for h in range(halves)], axis=1
        )

    def inner_transform(real, imag):
        high, low = split(jnp.concatenate([real, imag], axis=1))
        return dot(high, inner_v[0]) + dot(low, inner_v[0]) + dot(high, inner_v[1])

    def channel(chunk, c, carry):
        cosine, sine = turn[0], turn[1]
        signals = [
            column(rfh, chunk * GROUP * halves + c),
            column(rmd.at[chunk], c),
            column(rmd.at[chunk], GROUP * halves + c),
        ]
        high, low = split(jnp.concatenate(signals, axis=1))
        spread = dot(first[...], jnp.concatenate([high, low, high], axis=0))
        pairs = [
            turned(
                spread[:parts, s * width : (s + 1) * width],
                spread[parts:, s * width : (s + 1) * width],
                cosine, sine,
            )
            for s in range(3)
        ]
        spectra = inner_transform(
            jnp.concatenate([p[0] for p in pairs], axis=0),
            jnp.concatenate([p[1] for p in pairs], axis=0),
        )
        real, imag = spectra[:, :width], spectra[:, width:]
        sr, si = real[2 * parts :], imag[2 * parts :]
        both_r = [real[s * parts : (s + 1) * parts] * sr + imag[s * parts : (s + 1) * parts] * si for s in (0, 1)]
        both_i = [imag[s * parts : (s + 1) * parts] * sr - real[s * parts : (s + 1) * parts] * si for s in (0, 1)]
        back = inner_transform(jnp.concatenate(both_r, axis=0), jnp.concatenate(both_i, axis=0))
        pairs = [
            turned(back[s * parts : (s + 1) * parts, :width], back[s * parts : (s + 1) * parts, width:], cosine, sine)
            for s in (0, 1)
        ]
        folded = jnp.concatenate(
            [jnp.concatenate([p[0] for p in pairs], axis=1), jnp.concatenate([p[1] for p in pairs], axis=1)],
            axis=0,
        )
        high, low = split(folded)
        result = dot(last[...], jnp.concatenate([high, low, high], axis=0))
        gain = skip[me * rows + chunk * GROUP + c]
        both = (
            result[:, :width] + gain * signals[2],
            result[:, width:] * ((parts * width) ** -0.5),
        )
        for s in range(2):
            for h in range(halves):
                start = (s * halves + h) * GROUP + c
                res[chunk, pl.ds(start, parts, stride=tall), :] = both[s][
                    :, h * LANES : (h + 1) * LANES
                ]
        return carry

    for chunk in range(CHUNKS):
        arrived(rmd.at[chunk], 2 + chunk)
        lax.fori_loop(0, GROUP, functools.partial(channel, chunk), 0)
        send(res.at[chunk], out.at[chunk], 4 + chunk)

    keep.wait()
    done = cnt_all.at[pl.ds(0, parts - 1)]
    pltpu.make_async_copy(done, done, send_sem.at[0]).wait()
    sent(rf, 1)
    for chunk in range(CHUNKS):
        sent(rmd.at[chunk], 2 + chunk)
    for chunk in range(CHUNKS):
        sent(res.at[chunk], 4 + chunk)
        arrived(out.at[chunk], 4 + chunk)


def on_device(
    token_ids, domain_ids, domain_counts, embed_table, query_act, key_act, conv_saved,
    loss_seed, filters, skip_gain,
):
    parts = lax.axis_size("ctx")
    chans, width = query_act.shape
    vocab = embed_table.shape[0]
    first, inner, last, turn = [jnp.asarray(x) for x in constants(parts, width)]
    vmem = pl.BlockSpec(memory_space=pltpu.VMEM)
    smem = pl.BlockSpec(memory_space=pltpu.SMEM)
    hbm = pl.BlockSpec(memory_space=pl.ANY)
    rows = CHUNKS * GROUP
    halves = width // LANES
    assert chans == parts * rows
    out, values, weight = pl.pallas_call(
        functools.partial(kernel, parts, width),
        out_shape=(
            jax.ShapeDtypeStruct((CHUNKS, chans * halves, LANES), F32),
            jax.ShapeDtypeStruct((chans, width), F32),
            jax.ShapeDtypeStruct((1, width), F32),
        ),
        in_specs=[vmem, vmem, vmem, smem, vmem, vmem, vmem] + [hbm] * 6,
        out_specs=(hbm, hbm, vmem),
        scratch_shapes=[
            pltpu.VMEM((8, LANES), F32),
            pltpu.VMEM((parts, 8, LANES), F32),
            pltpu.VMEM((vocab, chans), BF16),
            pltpu.VMEM((chans, width), BF16),
            pltpu.VMEM((chans, width), BF16),
            pltpu.VMEM((chans, width), BF16),
            pltpu.VMEM(inner.shape, BF16),
            pltpu.VMEM((chans, width), F32),
            pltpu.VMEM((CHUNKS, chans * halves, LANES), F32),
            pltpu.VMEM((chans, width), F32),
            pltpu.VMEM((chans * halves, LANES), F32),
            pltpu.VMEM((CHUNKS, chans * halves, LANES), F32),
            pltpu.VMEM((CHUNKS, chans * halves, LANES), F32),
            pltpu.SemaphoreType.DMA((5,)),
            pltpu.SemaphoreType.DMA,
            pltpu.SemaphoreType.DMA((6,)),
            pltpu.SemaphoreType.DMA((6,)),
        ],
        compiler_params=pltpu.CompilerParams(
            collective_id=0, has_side_effects=True, vmem_limit_bytes=40 * 2**20
        ),
        name="exchange",
    )(
        domain_counts, token_ids[None, :], domain_ids[None, :], skip_gain, first, last, turn,
        embed_table, query_act, key_act, loss_seed, filters, inner,
    )
    sorted_out = out.reshape(CHUNKS, parts, 2, halves, GROUP, LANES).transpose(2, 1, 0, 4, 3, 5)
    back = sorted_out[0].reshape(chans, width)
    grad_filter = sorted_out[1].reshape(chans, width)
    rounded = (loss_seed.astype(F32) * weight).astype(BF16)
    upstream = lax.optimization_barrier(rounded).astype(F32)
    grad_query = upstream * conv_saved.astype(F32)
    return grad_query, back * values, back * key_act.astype(F32), grad_filter


def solution(mesh):
    in_specs = (
        P("ctx"), P("ctx"), P("ctx", None), P(None, "chan"),
        P("chan", "ctx"), P("chan", "ctx"), P("chan", "ctx"), P("chan", "ctx"), P("chan", "ctx"),
        P("chan"),
    )
    out_specs = (P("chan", "ctx"),) * 4
    return jax.shard_map(
        on_device, mesh=mesh, in_specs=in_specs, out_specs=out_specs, check_vma=False
    )
```

time: 388 us -> 146 us (0.38); the launches traced: 380 us -> 144 us
  blocking collectives: 166 us -> 0 us
  Pallas kernels: 0 us -> 128 us
  matrix products: 78.3 us -> 0 us
  waiting for transfers between devices: 56.5 us -> 0 us
  starting transfers between devices: 46.4 us -> 0 us
  local copies, waits for them, and re-layouts: 23.2 us -> 13.5 us
  other arithmetic: 8.57 us -> 1.9 us
    psum x1 -> x0, blocking collectives: 166 us -> none  [on_device(): totals = lax.psum(domain_counts.astype(jnp.float32), 'ctx')]
    pallas_call x0 -> x1, Pallas kernels: none -> 128 us  [on_device(): pl.pallas_call(functools.partial(kernel, parts, width), out_shape=(jax.Sh...]
    dot_general x19 -> x0, matrix products: 78.3 us -> none  [the longest x4 17.8 us: rotate(): return (product(real, cosine), sign * product(real, sine))]
    all_to_all x3 -> x0, waiting for transfers between devices: 56.5 us -> none  [the longest x2 30.9 us: ch_forward(): lax.all_to_all(signal.reshape(count, chans, 1, width), 'ctx', split_axis=...]
    all_to_all x3 -> x0, starting transfers between devices: 46.4 us -> none  [the longest x2 38.4 us: ch_forward(): lax.all_to_all(signal.reshape(count, chans, 1, width), 'ctx', split_axis=...]
    mul x4 -> x1, other arithmetic: 5.83 us -> 1.8 us  [on_device(): return (grad_query, back * values, back * key_act.astype(F32), grad_filter)]
    unnamed x53 -> x28, local copies, waits for them, and re-layouts: 13.3 us -> 12 us
  transfers between devices with their start and end apart: 3 -> 0, of which waited for: 3 -> 0; matrix products, arithmetic and copies ran while one was open for 7% -> 0% of each run, Pallas kernels for 0% -> 0%
where the time goes in v1:
time: 146 us; the launch traced here: 144 us
  Pallas kernels  128 us (88%)
  local copies, waits for them, and re-layouts  13.5 us (9%)
  other arithmetic  1.9 us (1%)
    pallas_call x1, Pallas kernels, on_device(): pl.pallas_call(functools.partial(kernel, parts, width), out_shape=(jax.Sh...  128 us
    unnamed x28, local copies, waits for them, and re-layouts  12 us

profile of v1, /device:TPU:192, one launch (start us, length us, event | category | flops | bytes accessed | tf_op | source)
XLA Modules:
  0.0 144.4 jit_solution(9325846252811589350)
XLA Ops:
  0.6 0.0 copy-start
  0.6 1.0 copy-done
  1.7 0.0 copy-start.1
  1.7 1.0 copy-done.1
  2.7 0.0 copy-start.2
  2.7 1.2 copy-done.2
  3.9 0.0 copy-start.3
  3.9 1.2 copy-done.3
  5.2 0.0 copy-start.4
  5.2 1.2 copy-done.4
  6.4 0.0 copy-start.5
  6.4 1.0 copy-done.5
  7.4 0.0 copy-start.6
  7.4 0.9 copy-done.6
  8.3 0.0 copy-start.7
  8.3 0.8 copy-done.7
  9.2 0.0 copy-start.8
  9.2 0.8 copy-done.8
  10.0 0.0 copy-start.9
  10.0 0.7 copy-done.9
  10.7 0.0 copy-start.10
  10.7 0.7 copy-done.10
  11.3 0.0 copy-start.11
  11.3 0.7 copy-done.11
  12.0 0.7 copy-done.12
  12.7 128.3 %exchange.1 = (f32[2,2048,128]{2,1,0:T(8,128)S(1)}, f32[1024,256]{1,0:T(8,128)S(1)}, f32[1,256]{1,0:T(1,128)S(1)}) custom-call(s32[1,8]{1,0:T(1,128)S(1)} %copy-done.12, s32[1,256]{1,0:T(1,128)S(1)} %bitcast.11, s32[1,256]{1,0:T(1,128)S(1)} %bitcast.12, f32[1024]{0:T(1024)S(1)} %copy-done.9, bf16[128,192]{1,0:T(8,128)(2,1)S(1)} %copy-done.7, ...), custom_call_target="tpu_custom_call" | custom-call | tf_op jit(solution)/shard_map/exchange/pallas_call | solution.py:293
  141.0 0.4 copy.20
  141.4 0.0 copy-start.13
  141.4 1.1 fusion
  142.5 0.1 multiply_convert_fusion
  142.6 0.0 copy-done.13
  142.6 1.8 %convert_multiply_fusion = (f32[1024,256]{1,0:T(8,128)}, f32[1024,256]{1,0:T(8,128)}, f32[1024,256]{1,0:T(8,128)}) fusion(f32[1024,256]{1,0:T(8,128)S(1)} %bitcast.14, bf16[1024,256]{1,0:T(8,128)(2,1)S(1)} %copy-done.1, f32[1024,256]{1,0:T(8,128)S(1)} %get-tuple-element.9, bf16[1024,256]{1,0:T(8,128)(2,1)S(1)} %copy-done.13, ...), kind=kLoop, calls=%fused_computation.1 | loop fusion | flops 1572864 | bytes 6815744 | tf_op jit(solution)/shard_map/mul | solution.py:335
  (1 shorter events, 0.0 us)
Async XLA Ops:
  0.6 1.0 copy-start
  1.7 1.0 copy-start.1
  2.7 1.2 copy-start.2
  3.9 1.2 copy-start.3
  5.2 1.2 copy-start.4
  6.4 1.0 copy-start.5
  7.4 0.9 copy-start.6
  8.3 0.8 copy-start.7
  9.2 0.8 copy-start.8
  10.0 0.7 copy-start.9
  10.7 0.7 copy-start.10
  11.3 0.7 copy-start.11
  12.0 0.7 copy-start.12
  141.4 1.3 copy-start.13

commit v2 on v1

--- a/solution.py
+++ b/solution.py
@@ -29,7 +29,6 @@
     theta = 2.0 * np.pi * np.outer(j + 0.25, j) / parts
     first = np.concatenate([np.cos(theta), -np.sin(theta)], 0)
     phase = 2.0 * np.pi * np.outer(j + 0.25, r) / total
-    turn = np.stack([np.cos(phase), np.sin(phase)]).astype(np.float32)
     omega = 2.0 * np.pi * (np.outer(r, r) % width) / width
     cosine, sine = np.cos(omega), np.sin(omega)
     inner = np.block([[cosine, -sine], [sine, cosine]])
@@ -38,7 +37,12 @@
     lh, ll = split_host(last)
     first_cat = np.concatenate([fh, fh, fl], 1)
     last_cat = np.concatenate([lh, lh, ll], 1)
-    return first_cat, np.stack(split_host(inner)), last_cat, turn
+    table = np.zeros((2 * width + 4 * parts, 2 * width), np.float32)
+    table[: 2 * width] = inner
+    table[2 * width : 2 * width + parts] = np.concatenate([np.cos(phase), np.sin(phase)], 1)
+    table[2 * width + parts : 2 * width + 3 * parts, : 3 * parts] = first_cat
+    table[2 * width + 3 * parts :, : 6 * parts] = last_cat
+    return table
 
 
 def split(x):
@@ -56,12 +60,14 @@
 
 def kernel(
     parts, width,
-    counts, tokens, domains, skip, first, last, turn,
-    embed, query, key, loss, filters, inner,
-    out, values_out, weight_out,
-    cnt_src, cnt_all, embed_v, query_v, key_v, loss_v, inner_v, values_v,
-    md, rf, rfh, rmd, res,
-    load_sem, keep_sem, send_sem, recv_sem,
+    counts, tokens, domains, skip, table,
+    embed, query, key, saved, loss, filters,
+    grad_query, grad_key, grad_value, grad_filter,
+    counts_v, tokens_v, domains_v, skip_s, table_v,
+    cnt_src, cnt_all, embed_v, query_v, key_v, saved_v, loss_v, first, last, inner_v,
+    values_v, keyed_v, out,
+    md, rf, rfh, rmd, res_h, res,
+    load_sem, send_sem, recv_sem,
 ):
     me = lax.axis_index("ctx")
     chan = lax.axis_index("chan")
@@ -80,27 +86,33 @@
     loads = [
         pltpu.make_async_copy(source, target, load_sem.at[i])
         for i, (source, target) in enumerate(
-            [(embed, embed_v), (key, key_v), (query, query_v), (loss, loss_v), (inner, inner_v)]
+            [
+                (counts, counts_v), (tokens, tokens_v), (domains, domains_v), (embed, embed_v),
+                (key, key_v), (query, query_v), (saved, saved_v), (loss, loss_v),
+                (skip, skip_s), (table, table_v),
+            ]
         )
     ]
     for load in loads:
         load.start()
+    domain_count = counts.shape[1]
     cnt_src[...] = jnp.zeros_like(cnt_src)
-    cnt_src[0:1, 0 : counts.shape[1]] = counts[...].astype(F32)
+    loads[0].wait()
+    cnt_src[0:1, 0:domain_count] = counts_v[...].astype(F32)
 
     def rows_of(ref, index):
         size = ref.shape[0] // parts
         return ref.at[pl.ds(pl.multiple_of(index * size, size), size)]
 
     def send(source, target, slot):
-        own = pltpu.make_async_copy(rows_of(source, me), rows_of(target, me), recv_sem.at[slot])
+        own = pltpu.make_async_copy(source(me), target(me), recv_sem.at[slot])
         own.start()
 
         def go(k, carry):
             peer = lax.rem(me + k, parts)
             pltpu.make_async_remote_copy(
-                src_ref=rows_of(source, peer),
-                dst_ref=rows_of(target, me),
+                src_ref=source(peer),
+                dst_ref=target(me),
                 send_sem=send_sem.at[slot],
                 recv_sem=recv_sem.at[slot],
                 device_id=(peer, chan),
@@ -119,28 +131,31 @@
 
     pl.semaphore_wait(barrier, parts - 1)
 
-    own = pltpu.make_async_copy(cnt_src, cnt_all.at[me], recv_sem.at[0])
-    own.start()
+    pltpu.make_async_copy(cnt_src, cnt_all.at[me], recv_sem.at[0]).start()
+    pltpu.make_async_copy(rows_of(filters, me), rows_of(rf, me), recv_sem.at[1]).start()
 
     def tell(k, carry):
         peer = lax.rem(me + k, parts)
-        pltpu.make_async_remote_copy(
-            src_ref=cnt_src,
-            dst_ref=cnt_all.at[me],
-            send_sem=send_sem.at[0],
-            recv_sem=recv_sem.at[0],
-            device_id=(peer, chan),
-            device_id_type=MESH,
-        ).start()
+        for slot, source, target in (
+            (0, cnt_src, cnt_all.at[me]), (1, rows_of(filters, peer), rows_of(rf, me)),
+        ):
+            pltpu.make_async_remote_copy(
+                src_ref=source,
+                dst_ref=target,
+                send_sem=send_sem.at[slot],
+                recv_sem=recv_sem.at[slot],
+                device_id=(peer, chan),
+                device_id_type=MESH,
+            ).start()
         return carry
 
     lax.fori_loop(1, parts, tell, 0)
-    send(filters, rf, 1)
-
-    loads[0].wait()
+
+    for load in loads[1:4]:
+        load.wait()
     vocab = embed_v.shape[0]
     onehot = (
-        lax.broadcasted_iota(jnp.int32, (vocab, width), 0) == tokens[...]
+        lax.broadcasted_iota(jnp.int32, (vocab, width), 0) == tokens_v[...]
     ).astype(F32).astype(BF16)
     piece = 128
 
@@ -153,23 +168,23 @@
         return carry
 
     lax.fori_loop(0, values_v.shape[0] // piece, look_up, 0)
-    keep = pltpu.make_async_copy(values_v, values_out, keep_sem)
-    keep.start()
-    for load in loads[1:4]:
+    for load in loads[4:8]:
         load.wait()
     arrived(cnt_all, 0)
-    totals = jnp.sum(cnt_all[...], axis=0)[0:1, :]
+    totals = jnp.sum(cnt_all[...], axis=0)
     shares = (count_unit * parts) / totals
     weight = jnp.zeros((1, width), F32)
-    for d in range(counts.shape[1]):
-        weight = jnp.where(domains[...] == d, shares[0:1, d : d + 1], weight)
-    weight_out[...] = weight
+    for d in range(domain_count):
+        weight = jnp.where(domains_v[...] == d, shares[0:1, d : d + 1], weight)
 
     def products(b, carry):
         at = pl.multiple_of(b * piece, piece)
         block = pl.ds(at, piece)
-        mixed = key_v[block, :].astype(F32) * values_v[block, :]
+        keyed = key_v[block, :].astype(F32)
+        keyed_v[block, :] = keyed
+        mixed = keyed * values_v[block, :]
         upstream = (loss_v[block, :].astype(F32) * weight).astype(BF16).astype(F32)
+        grad_query[block, :] = upstream * saved_v[block, :].astype(F32)
         dconv = upstream * query_v[block, :].astype(F32)
         for q in range(piece // rows):
             for chunk in range(CHUNKS):
@@ -184,9 +199,16 @@
 
     lax.fori_loop(0, values_v.shape[0] // piece, products, 0)
     for chunk in range(CHUNKS):
-        send(md.at[chunk], rmd.at[chunk], 2 + chunk)
-
-    loads[4].wait()
+        send(
+            lambda i: rows_of(md.at[chunk], i), lambda i: rows_of(rmd.at[chunk], i), 2 + chunk
+        )
+
+    for load in loads[8:]:
+        load.wait()
+    double = 2 * width
+    first[...] = table_v[double + parts : double + 3 * parts, 0 : 3 * parts].astype(BF16)
+    last[...] = table_v[double + 3 * parts : double + 4 * parts, 0 : 6 * parts].astype(BF16)
+    inner_v[0], inner_v[1] = split(table_v[0:double, :])
     arrived(rf, 1)
 
     def halve(b, carry):
@@ -212,7 +234,8 @@
         return dot(high, inner_v[0]) + dot(low, inner_v[0]) + dot(high, inner_v[1])
 
     def channel(chunk, c, carry):
-        cosine, sine = turn[0], turn[1]
+        cosine = table_v[double : double + parts, 0:width]
+        sine = table_v[double : double + parts, width:double]
         signals = [
             column(rfh, chunk * GROUP * halves + c),
             column(rmd.at[chunk], c),
@@ -247,33 +270,57 @@
         )
         high, low = split(folded)
         result = dot(last[...], jnp.concatenate([high, low, high], axis=0))
-        gain = skip[me * rows + chunk * GROUP + c]
-        both = (
-            result[:, :width] + gain * signals[2],
-            result[:, width:] * ((parts * width) ** -0.5),
-        )
+        gain = skip_s[me * rows + chunk * GROUP + c]
+        both = (result[:, :width] + gain * signals[2], result[:, width:])
         for s in range(2):
             for h in range(halves):
                 start = (s * halves + h) * GROUP + c
-                res[chunk, pl.ds(start, parts, stride=tall), :] = both[s][
+                res_h[pl.ds(start, parts, stride=tall), :] = both[s][
                     :, h * LANES : (h + 1) * LANES
                 ]
+        return carry
+
+    def widen(chunk, b, carry):
+        for q in range(4):
+            block = b * 4 + q
+            start = pl.multiple_of(block * tall, tall)
+            for s in range(2):
+                res[chunk, block, s] = jnp.concatenate(
+                    [
+                        res_h[pl.ds(start + (s * halves + h) * GROUP, GROUP), :]
+                        for h in range(halves)
+                    ],
+                    axis=1,
+                )
+        return carry
+
+    def finish(chunk, b, carry):
+        for q in range(4):
+            block = b * 4 + q
+            here = pl.ds(pl.multiple_of(block * rows + chunk * GROUP, GROUP), GROUP)
+            back = out[chunk, block, 0]
+            grad_key[here, :] = back * values_v[here, :]
+            grad_value[here, :] = back * keyed_v[here, :]
+            grad_filter[here, :] = out[chunk, block, 1] * ((parts * width) ** -0.5)
         return carry
 
     for chunk in range(CHUNKS):
         arrived(rmd.at[chunk], 2 + chunk)
         lax.fori_loop(0, GROUP, functools.partial(channel, chunk), 0)
-        send(res.at[chunk], out.at[chunk], 4 + chunk)
-
-    keep.wait()
+        lax.fori_loop(0, parts // 4, functools.partial(widen, chunk), 0)
+        send(lambda i: res.at[chunk, i], lambda i: out.at[chunk, i], 4 + chunk)
+
     done = cnt_all.at[pl.ds(0, parts - 1)]
     pltpu.make_async_copy(done, done, send_sem.at[0]).wait()
     sent(rf, 1)
     for chunk in range(CHUNKS):
         sent(rmd.at[chunk], 2 + chunk)
     for chunk in range(CHUNKS):
-        sent(res.at[chunk], 4 + chunk)
+        whole = res.at[chunk]
+        done = whole.at[pl.ds(0, parts - 1)]
+        pltpu.make_async_copy(done, done, send_sem.at[4 + chunk]).wait()
         arrived(out.at[chunk], 4 + chunk)
+        lax.fori_loop(0, parts // 4, functools.partial(finish, chunk), 0)
 
 
 def on_device(
@@ -283,38 +330,44 @@
     parts = lax.axis_size("ctx")
     chans, width = query_act.shape
     vocab = embed_table.shape[0]
-    first, inner, last, turn = [jnp.asarray(x) for x in constants(parts, width)]
+    table = jnp.asarray(constants(parts, width))
     vmem = pl.BlockSpec(memory_space=pltpu.VMEM)
-    smem = pl.BlockSpec(memory_space=pltpu.SMEM)
-    hbm = pl.BlockSpec(memory_space=pl.ANY)
+    hbm = pl.BlockSpec(memory_space=pltpu.HBM)
     rows = CHUNKS * GROUP
     halves = width // LANES
     assert chans == parts * rows
-    out, values, weight = pl.pallas_call(
+    hold = jax.ShapeDtypeStruct((chans, width), F32)
+    results = pl.pallas_call(
         functools.partial(kernel, parts, width),
-        out_shape=(
-            jax.ShapeDtypeStruct((CHUNKS, chans * halves, LANES), F32),
-            jax.ShapeDtypeStruct((chans, width), F32),
-            jax.ShapeDtypeStruct((1, width), F32),
-        ),
-        in_specs=[vmem, vmem, vmem, smem, vmem, vmem, vmem] + [hbm] * 6,
-        out_specs=(hbm, hbm, vmem),
+        out_shape=(hold,) * 4,
+        in_specs=[hbm] * 11,
+        out_specs=(vmem,) * 4,
         scratch_shapes=[
-            pltpu.VMEM((8, LANES), F32),
-            pltpu.VMEM((parts, 8, LANES), F32),
+            pltpu.VMEM(domain_counts.shape, jnp.int32),
+            pltpu.VMEM((1, width), jnp.int32),
+            pltpu.VMEM((1, width), jnp.int32),
+            pltpu.SMEM((chans,), F32),
+            pltpu.VMEM(table.shape, F32),
+            pltpu.VMEM((1, LANES), F32),
+            pltpu.VMEM((parts, 1, LANES), F32),
             pltpu.VMEM((vocab, chans), BF16),
             pltpu.VMEM((chans, width), BF16),
             pltpu.VMEM((chans, width), BF16),
             pltpu.VMEM((chans, width), BF16),
-            pltpu.VMEM(inner.shape, BF16),
+            pltpu.VMEM((chans, width), BF16),
+            pltpu.VMEM((2 * parts, 3 * parts), BF16),
+            pltpu.VMEM((parts, 6 * parts), BF16),
+            pltpu.VMEM((2, 2 * width, 2 * width), BF16),
             pltpu.VMEM((chans, width), F32),
+            pltpu.VMEM((chans, width), F32),
+            pltpu.VMEM((CHUNKS, parts, 2, GROUP, width), F32),
             pltpu.VMEM((CHUNKS, chans * halves, LANES), F32),
             pltpu.VMEM((chans, width), F32),
             pltpu.VMEM((chans * halves, LANES), F32),
             pltpu.VMEM((CHUNKS, chans * halves, LANES), F32),
-            pltpu.VMEM((CHUNKS, chans * halves, LANES), F32),
-            pltpu.SemaphoreType.DMA((5,)),
-            pltpu.SemaphoreType.DMA,
+            pltpu.VMEM((chans * halves, LANES), F32),
+            pltpu.VMEM((CHUNKS, parts, 2, GROUP, width), F32),
+            pltpu.SemaphoreType.DMA((10,)),
             pltpu.SemaphoreType.DMA((6,)),
             pltpu.SemaphoreType.DMA((6,)),
         ],
@@ -322,17 +375,33 @@
             collective_id=0, has_side_effects=True, vmem_limit_bytes=40 * 2**20
         ),
         name="exchange",
-    )(
-        domain_counts, token_ids[None, :], domain_ids[None, :], skip_gain, first, last, turn,
-        embed_table, query_act, key_act, loss_seed, filters, inner,
-    )
-    sorted_out = out.reshape(CHUNKS, parts, 2, halves, GROUP, LANES).transpose(2, 1, 0, 4, 3, 5)
-    back = sorted_out[0].reshape(chans, width)
-    grad_filter = sorted_out[1].reshape(chans, width)
-    rounded = (loss_seed.astype(F32) * weight).astype(BF16)
-    upstream = lax.optimization_barrier(rounded).astype(F32)
-    grad_query = upstream * conv_saved.astype(F32)
-    return grad_query, back * values, back * key_act.astype(F32), grad_filter
+    )(*[
+        pltpu.with_memory_space_constraint(x, pltpu.HBM)
+        for x in (
+            domain_counts, token_ids[None, :], domain_ids[None, :], skip_gain, table,
+            embed_table, query_act, key_act, conv_saved, loss_seed, filters,
+        )
+    ])
+    return pl.pallas_call(
+        write_out,
+        out_shape=(hold,) * 4,
+        in_specs=[pl.BlockSpec(memory_space=pl.ANY)] * 4,
+        out_specs=(hbm,) * 4,
+        scratch_shapes=[pltpu.SemaphoreType.DMA((4,))],
+        compiler_params=pltpu.CompilerParams(vmem_limit_bytes=4 * 2**20),
+        name="write_out",
+    )(*[pltpu.with_memory_space_constraint(x, pltpu.VMEM) for x in results])
+
+
+def write_out(*refs):
+    semaphores = refs[-1]
+    copies = [
+        pltpu.make_async_copy(refs[i], refs[4 + i], semaphores.at[i]) for i in range(4)
+    ]
+    for copy in copies:
+        copy.start()
+    for copy in copies:
+        copy.wait()
 
 
 def solution(mesh):

time: 146 us -> 130 us (0.89)
  the two profiles are of different devices: /device:TPU:192 before, /device:TPU:6 now
where the time goes in v2:
time: 130 us
  Pallas kernels  129 us (99%)
    pallas_call x1, Pallas kernels, on_device(): pl.pallas_call(functools.partial(kernel, parts, width), out_shape=(hold,)...  127 us

profile of v2, /device:TPU:6, one launch (start us, length us, event | category | flops | bytes accessed | tf_op | source)
XLA Modules:
  0.0 130.1 jit_solution(8329621356708798447)
XLA Ops:
  0.6 127.4 %exchange.1 = (f32[1024,256]{1,0:T(8,128)S(1)}, f32[1024,256]{1,0:T(8,128)S(1)}, f32[1024,256]{1,0:T(8,128)S(1)}, f32[1024,256]{1,0:T(8,128)S(1)}) custom-call(s32[1,8]{1,0:T(1,128)} %counts.1, s32[1,256]{1,0:T(1,128)} %bitcast.2, s32[1,256]{1,0:T(1,128)} %bitcast.3, f32[1024]{0:T(1024)} %skip.1, f32[768,512]{1,0:T(8,128)} %constant.2.clone.table, ...), custom_call_target="tpu_custom_call" | custom-call | tf_op jit(solution)/shard_map/exchange/pallas_call | solution.py:340
  128.0 2.0 %write_out.1 = (f32[1024,256]{1,0:T(8,128)}, f32[1024,256]{1,0:T(8,128)}, f32[1024,256]{1,0:T(8,128)}, f32[1024,256]{1,0:T(8,128)}) custom-call(f32[1024,256]{1,0:T(8,128)S(1)} %get-tuple-element.8.refs_0_, f32[1024,256]{1,0:T(8,128)S(1)} %get-tuple-element.9.refs_1_, f32[1024,256]{1,0:T(8,128)S(1)} %get-tuple-element.10.refs_2_, ...), custom_call_target="tpu_custom_call" | custom-call | tf_op jit(solution)/shard_map/write_out/pallas_call | solution.py:385

commit v3 on v2

v3 whole, which is shorter than its diff:
```python
import functools

import jax
import jax.numpy as jnp
import ml_dtypes
import numpy as np
from jax import lax
from jax.experimental import pallas as pl
from jax.experimental.pallas import tpu as pltpu
from jax.sharding import PartitionSpec as P

MESH = pl.DeviceIdType.MESH
F32, BF16 = jnp.float32, jnp.bfloat16
count_unit = 64.0
LANES = 128
GROUP = 8
CHUNKS = 2
BATCH = 4


def split_host(x):
    high = x.astype(np.float32).astype(ml_dtypes.bfloat16)
    low = (x - high.astype(np.float64)).astype(np.float32).astype(ml_dtypes.bfloat16)
    return high, low


def constants(parts, width):
    total = parts * width
    j, r = np.arange(parts), np.arange(width)
    theta = 2.0 * np.pi * np.outer(j + 0.25, j) / parts
    first = np.concatenate([np.cos(theta), -np.sin(theta)], 0)
    phase = 2.0 * np.pi * np.outer(j + 0.25, r) / total
    omega = 2.0 * np.pi * (np.outer(r, r) % width) / width
    cosine, sine = np.cos(omega), np.sin(omega)
    inner = np.block([[cosine, -sine], [sine, cosine]])
    last = np.concatenate([np.cos(theta).T, np.sin(theta).T], 1) / total
    fh, fl = split_host(first)
    lh, ll = split_host(last)
    first_cat = np.concatenate([fh, fh, fl], 1)
    last_cat = np.concatenate([lh, lh, ll], 1)
    table = np.zeros((2 * width + 4 * parts, 2 * width), np.float32)
    table[: 2 * width] = inner
    table[2 * width : 2 * width + parts] = np.concatenate([np.cos(phase), np.sin(phase)], 1)
    table[2 * width + parts : 2 * width + 3 * parts, : 3 * parts] = first_cat
    table[2 * width + 3 * parts :, : 6 * parts] = last_cat
    return table


def split(x):
    high = x.astype(BF16)
    return high, (x - high.astype(F32)).astype(BF16)


def dot(a, b):
    return jnp.dot(a, b, preferred_element_type=F32)


def turned(a, b, cosine, sine):
    return a * cosine + b * sine, b * cosine - a * sine


def kernel(
    parts, width, side,
    counts, tokens, domains, skip, table,
    embed, query, key, saved, loss, filters,
    grad_query, grad_key, grad_value, grad_filter,
    counts_v, tokens_v, domains_v, skip_s, table_v,
    cnt_src, cnt_z, cnt_part, cnt_all,
    embed_v, query_v, key_v, saved_v, loss_v, first, last, inner_v, values_v, keyed_v,
    md, zf, zmd, rf, rfh, rmd, res_h, res, zres, out,
    load_sem, send_sem, recv_sem,
):
    me = lax.axis_index("ctx")
    chan = lax.axis_index("chan")
    x, z, y = me // (side * side), lax.rem(me // side, side), lax.rem(me, side)
    plane = side * side
    rows = CHUNKS * GROUP
    halves = width // LANES
    tall = rows * halves
    steps = (2, 1, 3)
    barrier = pltpu.get_barrier_semaphore()

    def along(k):
        return lax.rem(z + k, side)

    def z_peer(k):
        return (x * plane + along(k) * side + y, chan)

    def beside(i):
        return lax.rem(x + i // side, side), lax.rem(y + i, side)

    def xy_peer(i):
        xx, yy = beside(i)
        return (xx * plane + z * side + yy, chan)

    def greet(i, carry):
        pl.semaphore_signal(barrier, inc=1, device_id=xy_peer(i), device_id_type=MESH)
        return carry

    for k in steps:
        pl.semaphore_signal(barrier, inc=1, device_id=z_peer(k), device_id_type=MESH)
    lax.fori_loop(1, plane, greet, 0)

    loads = [
        pltpu.make_async_copy(source, target, load_sem.at[i])
        for i, (source, target) in enumerate(
            [
                (counts, counts_v), (tokens, tokens_v), (domains, domains_v), (embed, embed_v),
                (key, key_v), (query, query_v), (saved, saved_v), (loss, loss_v),
                (skip, skip_s), (table, table_v),
            ]
        )
    ]
    for load in loads:
        load.start()
    domain_count = counts.shape[1]
    cnt_src[...] = jnp.zeros_like(cnt_src)
    loads[0].wait()
    cnt_src[0:1, 0:domain_count] = counts_v[...].astype(F32)

    def remote(source, target, slot, peer):
        pltpu.make_async_remote_copy(
            src_ref=source, dst_ref=target, send_sem=send_sem.at[slot], recv_sem=recv_sem.at[slot],
            device_id=peer, device_id_type=MESH,
        ).start()

    def spread_plane(source, target, slot):
        pltpu.make_async_copy(source(x, y), target, recv_sem.at[slot]).start()

        def go(i, carry):
            remote(source(*beside(i)), target, slot, xy_peer(i))
            return carry

        lax.fori_loop(1, plane, go, 0)

    def taken(like, slot, sem):
        pltpu.make_async_copy(like, like, sem.at[slot]).wait()

    def piece_of(ref, index, size):
        return ref.at[pl.ds(pl.multiple_of(index * size, size), size)]

    def source_index(k):
        return x * plane + lax.rem(z + side - k, side) * side + y

    cnt_slot, f_slot, md_slot, res_slot, end_slot = 0, (2, 22), (6, 10), (14, 17), (20, 21)

    pl.semaphore_wait(barrier, plane - 1 + side - 1)

    for k in steps:
        remote(cnt_src, cnt_z.at[k - 1], cnt_slot, z_peer(k))

    def send_filters(chunk):
        for k in steps:
            remote(
                filters.at[:, along(k), :, chunk], zf.at[chunk, k - 1], f_slot[chunk] + k, z_peer(k)
            )
        spread_plane(
            lambda xx, yy: filters.at[xx, z, yy, chunk],
            piece_of(rf.at[chunk], source_index(0), GROUP),
            f_slot[chunk],
        )

    def forward_filters(chunk, k):
        taken(zf.at[chunk, k - 1], f_slot[chunk] + k, recv_sem)
        spread_plane(
            lambda xx, yy: zf.at[chunk, k - 1, xx, yy],
            piece_of(rf.at[chunk], source_index(k), GROUP),
            f_slot[chunk],
        )

    send_filters(0)

    for load in loads[1:4]:
        load.wait()
    vocab = embed_v.shape[0]
    onehot = (
        lax.broadcasted_iota(jnp.int32, (vocab, width), 0) == tokens_v[...]
    ).astype(F32).astype(BF16)
    piece = 128

    def look_up(b, carry):
        at = pl.multiple_of(b * piece, piece)
        values_v[pl.ds(at, piece), :] = lax.dot_general(
            embed_v[:, pl.ds(at, piece)], onehot, (((0,), (0,)), ((), ())),
            preferred_element_type=F32,
        )
        return carry

    taken(cnt_z, cnt_slot, recv_sem)
    cnt_part[...] = cnt_src[...] + cnt_z[0] + cnt_z[1] + cnt_z[2]
    spread_plane(lambda xx, yy: cnt_part, cnt_all.at[x * side + y], cnt_slot + 1)
    lax.fori_loop(0, values_v.shape[0] // piece, look_up, 0)
    for load in loads[4:8]:
        load.wait()
    taken(cnt_all, cnt_slot + 1, recv_sem)
    totals = jnp.sum(cnt_all[...], axis=0)
    shares = (count_unit * parts) / totals
    weight = jnp.zeros((1, width), F32)
    for d in range(domain_count):
        weight = jnp.where(domains_v[...] == d, shares[0:1, d : d + 1], weight)

    def products(b, carry):
        at = pl.multiple_of(b * piece, piece)
        block = pl.ds(at, piece)
        keyed = key_v[block, :].astype(F32)
        keyed_v[block, :] = keyed
        mixed = keyed * values_v[block, :]
        upstream = (loss_v[block, :].astype(F32) * weight).astype(BF16).astype(F32)
        grad_query[block, :] = upstream * saved_v[block, :].astype(F32)
        dconv = upstream * query_v[block, :].astype(F32)
        for q in range(piece // rows):
            owner = b * (piece // rows) + q
            ox, oz, oy = owner // plane, lax.rem(owner // side, side), q % side
            for chunk in range(CHUNKS):
                part = slice(q * rows + chunk * GROUP, q * rows + (chunk + 1) * GROUP)
                for h in range(halves):
                    start = oy * tall + h * GROUP
                    lanes = slice(h * LANES, (h + 1) * LANES)
                    md[chunk, ox, oz, start : start + GROUP, :] = mixed[part, lanes]
                    start = start + halves * GROUP
                    md[chunk, ox, oz, start : start + GROUP, :] = dconv[part, lanes]
        return carry

    lax.fori_loop(0, values_v.shape[0] // piece, products, 0)

    def send_signals(chunk):
        for k in steps:
            remote(md.at[chunk, :, along(k)], zmd.at[chunk, k - 1], md_slot[chunk] + k, z_peer(k))
        spread_plane(
            lambda xx, yy: piece_of(md.at[chunk, xx, z], yy, tall),
            piece_of(rmd.at[chunk], source_index(0), tall),
            md_slot[chunk],
        )

    def forward_signals(chunk, k):
        taken(zmd.at[chunk, k - 1], md_slot[chunk] + k, recv_sem)
        spread_plane(
            lambda xx, yy: piece_of(zmd.at[chunk, k - 1, xx], yy, tall),
            piece_of(rmd.at[chunk], source_index(k), tall),
            md_slot[chunk],
        )

    send_signals(0)
    for k in steps:
        forward_filters(0, k)

    for load in loads[8:]:
        load.wait()
    double = 2 * width
    first[...] = table_v[double + parts : double + 3 * parts, 0 : 3 * parts].astype(BF16)
    last[...] = table_v[double + 3 * parts : double + 4 * parts, 0 : 6 * parts].astype(BF16)
    inner_v[0], inner_v[1] = split(table_v[0:double, :])
    for k in steps:
        forward_signals(0, k)
        if k == steps[1]:
            send_filters(1)
    send_signals(1)

    def halve(chunk, b, carry):
        at = pl.multiple_of(b * piece, piece)
        block = rf[chunk, pl.ds(at, piece), :]
        for q in range(piece // GROUP):
            for h in range(halves):
                start = pl.multiple_of((at + q * GROUP) * halves + h * GROUP, GROUP)
                rfh[chunk, pl.ds(start, GROUP), :] = block[
                    q * GROUP : (q + 1) * GROUP, h * LANES : (h + 1) * LANES
                ]
        return carry

    def column(ref, start, stride):
        return jnp.concatenate(
            [ref[pl.ds(start + h * GROUP, parts, stride=stride), :] for h in range(halves)], axis=1
        )

    def inner_transform(real, imag):
        high, low = split(jnp.concatenate([real, imag], axis=1))
        count = high.shape[0]
        coarse = dot(jnp.concatenate([high, low], axis=0), inner_v[0])
        return coarse[:count] + coarse[count:] + dot(high, inner_v[1])

    def channels(chunk, g, carry):
        cosine = table_v[double : double + parts, 0:width]
        sine = table_v[double : double + parts, width:double]
        lines = [[], [], []]
        for p in range(BATCH):
            c = g * BATCH + p
            lines[0].append(column(rfh.at[chunk], c, GROUP * halves))
            lines[1].append(column(rmd.at[chunk], c, tall))
            lines[2].append(column(rmd.at[chunk], GROUP * halves + c, tall))
        turns = [[], [], []]
        for p in range(BATCH):
            high, low = split(jnp.concatenate([line[p] for line in lines], axis=1))
            spread = dot(first[...], jnp.concatenate([high, low, high], axis=0))
            for s in range(3):
                turns[s].append(
                    turned(
                        spread[:parts, s * width : (s + 1) * width],
                        spread[parts:, s * width : (s + 1) * width],
                        cosine, sine,
                    )
                )
        flat = turns[0] + turns[1] + turns[2]
        spectra = inner_transform(
            jnp.concatenate([t[0] for t in flat], axis=0),
            jnp.concatenate([t[1] for t in flat], axis=0),
        )
        real, imag = spectra[:, :width], spectra[:, width:]
        batch = BATCH * parts
        sr, si = real[2 * batch :], imag[2 * batch :]
        both_r = [real[s * batch : (s + 1) * batch] * sr + imag[s * batch : (s + 1) * batch] * si for s in (0, 1)]
        both_i = [imag[s * batch : (s + 1) * batch] * sr - real[s * batch : (s + 1) * batch] * si for s in (0, 1)]
        back = inner_transform(jnp.concatenate(both_r, axis=0), jnp.concatenate(both_i, axis=0))
        for p in range(BATCH):
            pairs = []
            for s in (0, 1):
                at = s * batch + p * parts
                pairs.append(turned(back[at : at + parts, :width], back[at : at + parts, width:], cosine, sine))
            folded = jnp.concatenate(
                [jnp.concatenate([t[0] for t in pairs], axis=1), jnp.concatenate([t[1] for t in pairs], axis=1)],
                axis=0,
            )
            high, low = split(folded)
            result = dot(last[...], jnp.concatenate([high, low, high], axis=0))
            c = g * BATCH + p
            gain = skip_s[me * rows + chunk * GROUP + c]
            both = (result[:, :width] + gain * lines[2][p], result[:, width:])
            for s in range(2):
                for h in range(halves):
                    start = (s * halves + h) * GROUP + c
                    res_h[pl.ds(start, parts, stride=tall), :] = both[s][
                        :, h * LANES : (h + 1) * LANES
                    ]
        return carry

    def widen(chunk, zz, xx, carry):
        for yy in range(side):
            start = pl.multiple_of((xx * plane + zz * side + yy) * tall, tall)
            for s in range(2):
                res[chunk, xx, zz, yy, s] = jnp.concatenate(
                    [
                        res_h[pl.ds(start + (s * halves + h) * GROUP, GROUP), :]
                        for h in range(halves)
                    ],
                    axis=1,
                )
        return carry

    def finish(chunk, b, carry):
        for q in range(side):
            here = pl.ds(pl.multiple_of((b * side + q) * rows + chunk * GROUP, GROUP), GROUP)
            ox, oz = b // side, lax.rem(b, side)
            back = out[chunk, ox, oz, q, 0]
            grad_key[here, :] = back * values_v[here, :]
            grad_value[here, :] = back * keyed_v[here, :]
            grad_filter[here, :] = out[chunk, ox, oz, q, 1] * ((parts * width) ** -0.5)
        return carry

    def transform(chunk):
        taken(rf.at[chunk], f_slot[chunk], recv_sem)
        lax.fori_loop(0, rf.shape[1] // piece, functools.partial(halve, chunk), 0)
        taken(rmd.at[chunk], md_slot[chunk], recv_sem)
        lax.fori_loop(0, GROUP // BATCH, functools.partial(channels, chunk), 0)
        for k in steps + (0,):
            zz = along(k)
            lax.fori_loop(0, side, functools.partial(widen, chunk, zz), 0)
            spread_plane(
                lambda xx, yy: res.at[chunk, xx, zz, yy],
                zres.at[chunk, k - 1, x, y] if k else out.at[chunk, x, z, y],
                res_slot[chunk] + k - 1 if k else end_slot[chunk],
            )

    def forward_results(chunk, k):
        taken(zres.at[chunk, k - 1], res_slot[chunk] + k - 1, recv_sem)
        remote(zres.at[chunk, k - 1], out.at[chunk, :, z], end_slot[chunk], z_peer(k))

    transform(0)
    for k in steps:
        forward_filters(1, k)
    for k in steps:
        forward_signals(1, k)
        forward_results(0, k)
    transform(1)
    for k in steps:
        forward_results(1, k)

    taken(cnt_z, cnt_slot, send_sem)
    taken(cnt_all.at[pl.ds(0, plane - 1)], cnt_slot + 1, send_sem)
    for chunk in range(CHUNKS):
        for k in steps:
            taken(zf.at[chunk, k - 1], f_slot[chunk] + k, send_sem)
            taken(zmd.at[chunk, k - 1], md_slot[chunk] + k, send_sem)
            taken(rmd.at[chunk, pl.ds(0, (plane - 1) * tall)], res_slot[chunk] + k - 1, send_sem)
        taken(rf.at[chunk, pl.ds(0, (parts - side) * GROUP)], f_slot[chunk], send_sem)
        taken(rmd.at[chunk, pl.ds(0, (parts - side) * tall)], md_slot[chunk], send_sem)
    for chunk in range(CHUNKS):
        taken(out.at[chunk], end_slot[chunk], recv_sem)
        lax.fori_loop(0, plane, functools.partial(finish, chunk), 0)
    for chunk in range(CHUNKS):
        taken(rmd.at[chunk, pl.ds(0, (parts - 1) * tall)], end_slot[chunk], send_sem)


def on_device(
    token_ids, domain_ids, domain_counts, embed_table, query_act, key_act, conv_saved,
    loss_seed, filters, skip_gain,
):
    parts = lax.axis_size("ctx")
    chans, width = query_act.shape
    vocab = embed_table.shape[0]
    table = jnp.asarray(constants(parts, width))
    vmem = pl.BlockSpec(memory_space=pltpu.VMEM)
    hbm = pl.BlockSpec(memory_space=pltpu.HBM)
    rows = CHUNKS * GROUP
    halves = width // LANES
    side = 4
    assert chans == parts * rows and parts == side**3
    block = (2, GROUP, width)
    hold = jax.ShapeDtypeStruct((chans, width), F32)
    results = pl.pallas_call(
        functools.partial(kernel, parts, width, side),
        out_shape=(hold,) * 4,
        in_specs=[hbm] * 11,
        out_specs=(vmem,) * 4,
        scratch_shapes=[
            pltpu.VMEM(domain_counts.shape, jnp.int32),
            pltpu.VMEM((1, width), jnp.int32),
            pltpu.VMEM((1, width), jnp.int32),
            pltpu.SMEM((chans,), F32),
            pltpu.VMEM(table.shape, F32),
            pltpu.VMEM((1, LANES), F32),
            pltpu.VMEM((side - 1, 1, LANES), F32),
            pltpu.VMEM((1, LANES), F32),
            pltpu.VMEM((side**2, 1, LANES), F32),
            pltpu.VMEM((vocab, chans), BF16),
            pltpu.VMEM((chans, width), BF16),
            pltpu.VMEM((chans, width), BF16),
            pltpu.VMEM((chans, width), BF16),
            pltpu.VMEM((chans, width), BF16),
            pltpu.VMEM((2 * parts, 3 * parts), BF16),
            pltpu.VMEM((parts, 6 * parts), BF16),
            pltpu.VMEM((2, 2 * width, 2 * width), BF16),
            pltpu.VMEM((chans, width), F32),
            pltpu.VMEM((chans, width), F32),
            pltpu.VMEM((CHUNKS, side, side, side * rows * halves, LANES), F32),
            pltpu.VMEM((CHUNKS, side - 1, side, side, GROUP, width), F32),
            pltpu.VMEM((CHUNKS, side - 1, side, side * rows * halves, LANES), F32),
            pltpu.VMEM((CHUNKS, parts * GROUP, width), F32),
            pltpu.VMEM((CHUNKS, parts * GROUP * halves, LANES), F32),
            pltpu.VMEM((CHUNKS, chans * halves, LANES), F32),
            pltpu.VMEM((chans * halves, LANES), F32),
            pltpu.VMEM((CHUNKS, side, side, side) + block, F32),
            pltpu.VMEM((CHUNKS, side - 1, side, side) + block, F32),
            pltpu.VMEM((CHUNKS, side, side, side) + block, F32),
            pltpu.SemaphoreType.DMA((10,)),
            pltpu.SemaphoreType.DMA((26,)),
            pltpu.SemaphoreType.DMA((26,)),
        ],
        compiler_params=pltpu.CompilerParams(
            collective_id=0, has_side_effects=True, vmem_limit_bytes=44 * 2**20
        ),
        name="exchange",
    )(*[
        pltpu.with_memory_space_constraint(x, pltpu.HBM)
        for x in (
            domain_counts, token_ids[None, :], domain_ids[None, :], skip_gain, table,
            embed_table, query_act, key_act, conv_saved, loss_seed,
            filters.reshape(side, side, side, CHUNKS, GROUP, width),
        )
    ])
    return pl.pallas_call(
        write_out,
        out_shape=(hold,) * 4,
        in_specs=[pl.BlockSpec(memory_space=pl.ANY)] * 4,
        out_specs=(hbm,) * 4,
        scratch_shapes=[pltpu.SemaphoreType.DMA((4,))],
        compiler_params=pltpu.CompilerParams(vmem_limit_bytes=4 * 2**20),
        name="write_out",
    )(*[pltpu.with_memory_space_constraint(x, pltpu.VMEM) for x in results])


def write_out(*refs):
    semaphores = refs[-1]
    copies = [
        pltpu.make_async_copy(refs[i], refs[4 + i], semaphores.at[i]) for i in range(4)
    ]
    for copy in copies:
        copy.start()
    for copy in copies:
        copy.wait()


def solution(mesh):
    in_specs = (
        P("ctx"), P("ctx"), P("ctx", None), P(None, "chan"),
        P("chan", "ctx"), P("chan", "ctx"), P("chan", "ctx"), P("chan", "ctx"), P("chan", "ctx"),
        P("chan"),
    )
    out_specs = (P("chan", "ctx"),) * 4
    return jax.shard_map(
        on_device, mesh=mesh, in_specs=in_specs, out_specs=out_specs, check_vma=False
    )
```

time: 130 us -> 127 us (0.977)
  the two profiles are of different devices: /device:TPU:6 before, /device:TPU:192 now
where the time goes in v3:
time: 127 us; the launch traced here: 124 us
  Pallas kernels  124 us (98%)
    pallas_call x1, Pallas kernels, on_device(): pl.pallas_call(functools.partial(kernel, parts, width, side), out_shape=(...  122 us

profile of v3, /device:TPU:192, one launch (start us, length us, event | category | flops | bytes accessed | tf_op | source)
XLA Modules:
  0.0 124.4 jit_solution(1188388300680125165)
XLA Ops:
  0.6 121.7 %exchange.1 = (f32[1024,256]{1,0:T(8,128)S(1)}, f32[1024,256]{1,0:T(8,128)S(1)}, f32[1024,256]{1,0:T(8,128)S(1)}, f32[1024,256]{1,0:T(8,128)S(1)}) custom-call(s32[1,8]{1,0:T(1,128)} %counts.1, s32[1,256]{1,0:T(1,128)} %bitcast.4, s32[1,256]{1,0:T(1,128)} %bitcast.5, f32[1024]{0:T(1024)} %skip.1, f32[768,512]{1,0:T(8,128)} %constant.2.clone.table, ...), custom_call_target="tpu_custom_call" | custom-call | tf_op jit(solution)/shard_map/exchange/pallas_call | solution.py:418
  122.4 2.0 %write_out.1 = (f32[1024,256]{1,0:T(8,128)}, f32[1024,256]{1,0:T(8,128)}, f32[1024,256]{1,0:T(8,128)}, f32[1024,256]{1,0:T(8,128)}) custom-call(f32[1024,256]{1,0:T(8,128)S(1)} %get-tuple-element.8.refs_0_, f32[1024,256]{1,0:T(8,128)S(1)} %get-tuple-element.9.refs_1_, f32[1024,256]{1,0:T(8,128)S(1)} %get-tuple-element.10.refs_2_, ...), custom_call_target="tpu_custom_call" | custom-call | tf_op jit(solution)/shard_map/write_out/pallas_call | solution.py:469

commit v4 on v3

--- a/solution.py
+++ b/solution.py
@@ -77,7 +77,7 @@
     rows = CHUNKS * GROUP
     halves = width // LANES
     tall = rows * halves
-    steps = (2, 1, 3)
+    steps = (1, 2, 3)
     barrier = pltpu.get_barrier_semaphore()
 
     def along(k):
@@ -142,7 +142,7 @@
     def source_index(k):
         return x * plane + lax.rem(z + side - k, side) * side + y
 
-    cnt_slot, f_slot, md_slot, res_slot, end_slot = 0, (2, 22), (6, 10), (14, 17), (20, 21)
+    cnt_slot, f_slot, md_slot, res_slot, end_slot = 0, (2, 22), (6, 10), (14, 17), (26, 27)
 
     pl.semaphore_wait(barrier, plane - 1 + side - 1)
 
@@ -345,10 +345,11 @@
                 )
         return carry
 
-    def finish(chunk, b, carry):
+    def finish(chunk, oz, ox, carry):
         for q in range(side):
-            here = pl.ds(pl.multiple_of((b * side + q) * rows + chunk * GROUP, GROUP), GROUP)
-            ox, oz = b // side, lax.rem(b, side)
+            here = pl.ds(
+                pl.multiple_of(((ox * side + oz) * side + q) * rows + chunk * GROUP, GROUP), GROUP
+            )
             back = out[chunk, ox, oz, q, 0]
             grad_key[here, :] = back * values_v[here, :]
             grad_value[here, :] = back * keyed_v[here, :]
@@ -371,7 +372,7 @@
 
     def forward_results(chunk, k):
         taken(zres.at[chunk, k - 1], res_slot[chunk] + k - 1, recv_sem)
-        remote(zres.at[chunk, k - 1], out.at[chunk, :, z], end_slot[chunk], z_peer(k))
+        remote(zres.at[chunk, k - 1], out.at[chunk, :, z], end_slot[chunk] + 2 * k, z_peer(k))
 
     transform(0)
     for k in steps:
@@ -393,10 +394,14 @@
         taken(rf.at[chunk, pl.ds(0, (parts - side) * GROUP)], f_slot[chunk], send_sem)
         taken(rmd.at[chunk, pl.ds(0, (parts - side) * tall)], md_slot[chunk], send_sem)
     for chunk in range(CHUNKS):
-        taken(out.at[chunk], end_slot[chunk], recv_sem)
-        lax.fori_loop(0, plane, functools.partial(finish, chunk), 0)
+        for k in (0,) + steps:
+            oz = lax.rem(z + side - k, side)
+            taken(out.at[chunk, :, oz], end_slot[chunk] + 2 * k, recv_sem)
+            lax.fori_loop(0, side, functools.partial(finish, chunk, oz), 0)
     for chunk in range(CHUNKS):
-        taken(rmd.at[chunk, pl.ds(0, (parts - 1) * tall)], end_slot[chunk], send_sem)
+        taken(rmd.at[chunk, pl.ds(0, (plane - 1) * tall)], end_slot[chunk], send_sem)
+        for k in steps:
+            taken(zres.at[chunk, k - 1], end_slot[chunk] + 2 * k, send_sem)
 
 
 def on_device(
@@ -451,8 +456,8 @@
             pltpu.VMEM((CHUNKS, side - 1, side, side) + block, F32),
             pltpu.VMEM((CHUNKS, side, side, side) + block, F32),
             pltpu.SemaphoreType.DMA((10,)),
-            pltpu.SemaphoreType.DMA((26,)),
-            pltpu.SemaphoreType.DMA((26,)),
+            pltpu.SemaphoreType.DMA((34,)),
+            pltpu.SemaphoreType.DMA((34,)),
         ],
         compiler_params=pltpu.CompilerParams(
             collective_id=0, has_side_effects=True, vmem_limit_bytes=44 * 2**20

time: 127 us -> 126 us (level); the launches traced: 124 us -> 125 us
  no operation moved by 1% of the time
where the time goes in v4:
time: 126 us; the launch traced here: 125 us
  Pallas kernels  125 us (99%)
    pallas_call x1, Pallas kernels, on_device(): pl.pallas_call(functools.partial(kernel, parts, width, side), out_shape=(...  123 us

profile of v4, /device:TPU:192, one launch (start us, length us, event | category | flops | bytes accessed | tf_op | source)
XLA Modules:
  0.0 125.5 jit_solution(11162885513554711320)
XLA Ops:
  0.6 122.8 %exchange.1 = (f32[1024,256]{1,0:T(8,128)S(1)}, f32[1024,256]{1,0:T(8,128)S(1)}, f32[1024,256]{1,0:T(8,128)S(1)}, f32[1024,256]{1,0:T(8,128)S(1)}) custom-call(s32[1,8]{1,0:T(1,128)} %counts.1, s32[1,256]{1,0:T(1,128)} %bitcast.4, s32[1,256]{1,0:T(1,128)} %bitcast.5, f32[1024]{0:T(1024)} %skip.1, f32[768,512]{1,0:T(8,128)} %constant.2.clone.table, ...), custom_call_target="tpu_custom_call" | custom-call | tf_op jit(solution)/shard_map/exchange/pallas_call | solution.py:423
  123.4 2.0 %write_out.1 = (f32[1024,256]{1,0:T(8,128)}, f32[1024,256]{1,0:T(8,128)}, f32[1024,256]{1,0:T(8,128)}, f32[1024,256]{1,0:T(8,128)}) custom-call(f32[1024,256]{1,0:T(8,128)S(1)} %get-tuple-element.8.refs_0_, f32[1024,256]{1,0:T(8,128)S(1)} %get-tuple-element.9.refs_1_, f32[1024,256]{1,0:T(8,128)S(1)} %get-tuple-element.10.refs_2_, ...), custom_call_target="tpu_custom_call" | custom-call | tf_op jit(solution)/shard_map/write_out/pallas_call | solution.py:474

commit v5 on v4

--- a/solution.py
+++ b/solution.py
@@ -93,6 +93,9 @@
         xx, yy = beside(i)
         return (xx * plane + z * side + yy, chan)
 
+    fetch = pltpu.make_async_copy(counts, counts_v, load_sem.at[9])
+    fetch.start()
+
     def greet(i, carry):
         pl.semaphore_signal(barrier, inc=1, device_id=xy_peer(i), device_id_type=MESH)
         return carry
@@ -101,21 +104,9 @@
         pl.semaphore_signal(barrier, inc=1, device_id=z_peer(k), device_id_type=MESH)
     lax.fori_loop(1, plane, greet, 0)
 
-    loads = [
-        pltpu.make_async_copy(source, target, load_sem.at[i])
-        for i, (source, target) in enumerate(
-            [
-                (counts, counts_v), (tokens, tokens_v), (domains, domains_v), (embed, embed_v),
-                (key, key_v), (query, query_v), (saved, saved_v), (loss, loss_v),
-                (skip, skip_s), (table, table_v),
-            ]
-        )
-    ]
-    for load in loads:
-        load.start()
     domain_count = counts.shape[1]
     cnt_src[...] = jnp.zeros_like(cnt_src)
-    loads[0].wait()
+    fetch.wait()
     cnt_src[0:1, 0:domain_count] = counts_v[...].astype(F32)
 
     def remote(source, target, slot, peer):
@@ -154,6 +145,8 @@
             remote(
                 filters.at[:, along(k), :, chunk], zf.at[chunk, k - 1], f_slot[chunk] + k, z_peer(k)
             )
+
+    def send_filters_plane(chunk):
         spread_plane(
             lambda xx, yy: filters.at[xx, z, yy, chunk],
             piece_of(rf.at[chunk], source_index(0), GROUP),
@@ -169,8 +162,21 @@
         )
 
     send_filters(0)
-
-    for load in loads[1:4]:
+    loads = [
+        pltpu.make_async_copy(source, target, load_sem.at[i])
+        for i, (source, target) in enumerate(
+            [
+                (tokens, tokens_v), (domains, domains_v), (embed, embed_v), (key, key_v),
+                (query, query_v), (saved, saved_v), (loss, loss_v), (skip, skip_s),
+                (table, table_v),
+            ]
+        )
+    ]
+    for load in loads:
+        load.start()
+    send_filters_plane(0)
+
+    for load in loads[0:3]:
         load.wait()
     vocab = embed_v.shape[0]
     onehot = (
@@ -190,7 +196,7 @@
     cnt_part[...] = cnt_src[...] + cnt_z[0] + cnt_z[1] + cnt_z[2]
     spread_plane(lambda xx, yy: cnt_part, cnt_all.at[x * side + y], cnt_slot + 1)
     lax.fori_loop(0, values_v.shape[0] // piece, look_up, 0)
-    for load in loads[4:8]:
+    for load in loads[3:7]:
         load.wait()
     taken(cnt_all, cnt_slot + 1, recv_sem)
     totals = jnp.sum(cnt_all[...], axis=0)
@@ -244,7 +250,7 @@
     for k in steps:
         forward_filters(0, k)
 
-    for load in loads[8:]:
+    for load in loads[7:]:
         load.wait()
     double = 2 * width
     first[...] = table_v[double + parts : double + 3 * parts, 0 : 3 * parts].astype(BF16)
@@ -254,6 +260,7 @@
         forward_signals(0, k)
         if k == steps[1]:
             send_filters(1)
+            send_filters_plane(1)
     send_signals(1)
 
     def halve(chunk, b, carry):

time: 126 us -> 126 us (level)
  no operation moved by 1% of the time
where the time goes in v5:
time: 126 us; the launch traced here: 125 us
  Pallas kernels  125 us (99%)
    pallas_call x1, Pallas kernels, on_device(): pl.pallas_call(functools.partial(kernel, parts, width, side), out_shape=(...  123 us

profile of v5, /device:TPU:192, one launch (start us, length us, event | category | flops | bytes accessed | tf_op | source)
XLA Modules:
  0.0 125.5 jit_solution(2492778599856105660)
XLA Ops:
  0.6 122.8 %exchange.1 = (f32[1024,256]{1,0:T(8,128)S(1)}, f32[1024,256]{1,0:T(8,128)S(1)}, f32[1024,256]{1,0:T(8,128)S(1)}, f32[1024,256]{1,0:T(8,128)S(1)}) custom-call(s32[1,8]{1,0:T(1,128)} %counts.1, s32[1,256]{1,0:T(1,128)} %bitcast.4, s32[1,256]{1,0:T(1,128)} %bitcast.5, f32[1024]{0:T(1024)} %skip.1, f32[768,512]{1,0:T(8,128)} %constant.2.clone.table, ...), custom_call_target="tpu_custom_call" | custom-call | tf_op jit(solution)/shard_map/exchange/pallas_call | solution.py:430
  123.4 2.0 %write_out.1 = (f32[1024,256]{1,0:T(8,128)}, f32[1024,256]{1,0:T(8,128)}, f32[1024,256]{1,0:T(8,128)}, f32[1024,256]{1,0:T(8,128)}) custom-call(f32[1024,256]{1,0:T(8,128)S(1)} %get-tuple-element.8.refs_0_, f32[1024,256]{1,0:T(8,128)S(1)} %get-tuple-element.9.refs_1_, f32[1024,256]{1,0:T(8,128)S(1)} %get-tuple-element.10.refs_2_, ...), custom_call_target="tpu_custom_call" | custom-call | tf_op jit(solution)/shard_map/write_out/pallas_call | solution.py:481
